TPU v7x, 256 devices: a whole 4x4x8 slice. The times are simulated.
256 devices in a mesh: state: 8 (over z_lo, y), snap: 32 (over x, z_hi, core).
Axes of the slice: x: 4, y: 4, z: 8 (z_hi: 4, z_lo: 2; z = z_hi * 2 + z_lo), core: 2. Of those that a mesh axis runs over, the one named last changes fastest.
Arguments:
- snapshots: bfloat16 [1024, 393216], P('snap', 'state'), may hold values from -64 to 64
- coefficients: bfloat16 [1024, 128], replicated, may hold values from -0.1875 to 0.1875
Outputs:
- gram: float32 [1024, 1024], P('snap', 'state')
- modes: float32 [393216, 128], P(('state', 'snap'))
All inputs are finite; a program needn't handle non-finite values.
Results may differ from a plain program's by a relative error of at most 0.0003.
Values may be sent and summed in bfloat16 or wider, within the bound.
No kernel may reach another device: no remote copies, remote signals or barrier semaphores. Data moves between devices by JAX's collectives and lax.ppermute only.
A program may use at most 64 MiB of HBM per device.

v0:
```python
import jax
import jax.numpy as jnp
from jax import lax
from jax.sharding import PartitionSpec as P

NS = 1024


def body(snapshots, coefficients):
    width = snapshots.shape[0]
    count = snapshots.shape[1]
    parts = lax.axis_size("snap")
    stripes = lax.axis_size("state")
    column = lax.axis_index("snap")
    stripe = lax.axis_index("state")
    total = NS
    col_width = total // stripes
    sub_rows = count // parts
    row_block = lax.all_to_all(snapshots, "snap", split_axis=1, concat_axis=0, tiled=True)
    raw = lax.dot_general(
        row_block, coefficients, (((0,), (0,)), ((), ())), preferred_element_type=jnp.float32
    )
    left = row_block.reshape(parts, width, sub_rows)
    right = row_block.reshape(stripes, col_width, sub_rows)
    blocks = jnp.einsum("pir,scr->spic", left, right, preferred_element_type=jnp.float32)
    blocks = blocks.reshape(stripes * parts * width, col_width)
    tile = lax.psum_scatter(blocks, ("state", "snap"), scatter_dimension=0, tiled=True)
    all_rows = count * stripes
    gram = tile / all_rows
    weights = coefficients.astype(jnp.float32)
    col_weights = lax.dynamic_slice_in_dim(weights, stripe * col_width, col_width, 0)
    row_weights = lax.dynamic_slice_in_dim(weights, column * width, width, 0)
    partial_energy = jnp.sum(
        jnp.dot(tile, col_weights, precision=lax.Precision.HIGHEST) * row_weights, axis=0
    )
    energy = lax.psum(partial_energy, ("state", "snap"))
    modes = raw * lax.rsqrt(energy / all_rows + 1e-06)
    return (gram, modes)


def solution(mesh):
    return jax.shard_map(
        body,
        mesh=mesh,
        in_specs=(P("snap", "state"), P()),
        out_specs=(P("snap", "state"), P(("state", "snap"), None)),
        check_vma=False,
    )
```

profile of v0, /device:TPU:1, one launch (start us, length us, event | category | flops | bytes accessed | tf_op | source)
XLA Modules:
  0.0 1685.3 jit_solution(6816694340039380033)
XLA Ops:
  7.2 0.0 reduce-scatter.2.cloned.1.call-start
  7.2 2.3 copy.8
  9.5 86.2 %all_to_all.19 = bf16[32,32,1536]{2,0,1:T(8,128)(2,1)S(1)} all-to-all(bf16[32,32,1536]{2,0,1:T(8,128)(2,1)S(1)} %bitcast.26), channel_id=1, replica_groups=mesh['state'=8,'snap'=32] {'snap'}, dimensions={1} | all-to-all | bytes 6291456 | tf_op jit(solution)/shard_map/all_to_all | solution.py:19
  95.7 5.1 fusion
  100.7 0.0 copy-start
  100.7 0.0 reduce-scatter.2.cloned.1.call-update
  100.8 1265.1 %reduce-scatter.2.cloned.1.call-done = f32[32,128]{1,0:T(8,128)} async-done(((f32[8192,128]{1,0:T(8,128)}), f32[32,128]{1,0:T(8,128)}) %reduce-scatter.2.cloned.1.call-update) | async-done | bytes 16400 | tf_op jit(solution)/shard_map/reduce_scatter | solution.py:27
  1365.9 0.0 copy-done
  1365.9 0.0 copy-start.1
  1365.9 0.9 fusion.2
  1366.8 309.0 %psum.7 = f32[128]{0:T(128)S(1)} all-reduce(f32[128]{0:T(128)S(1)} %fusion.2), channel_id=1, replica_groups=mesh['state'=8,'snap'=32] {'state','snap'}, use_global_device_ids=true, to_apply=%region_2.0 | all-reduce | flops 128 | bytes 1024 | tf_op jit(solution)/shard_map/psum | solution.py:36
  1675.9 1.9 convolution_multiply_fusion
  1677.8 0.0 copy-done.1
  1677.8 0.6 broadcast_multiply_fusion
  (1 shorter events, 0.0 us)
Async XLA Ops:
  7.2 1358.7 %reduce-scatter.2.cloned.1.call-start = ((), (), s32[]{:S(2)}) async-start(), calls=%async_computation.2 | async-start | bytes 4210688 | tf_op jit(solution)/shard_map/reduce_scatter | solution.py:27
  100.7 1265.1 %copy-start = (bf16[1024,128]{1,0:T(8,128)(2,1)S(1)}, bf16[1024,128]{1,0:T(8,128)(2,1)}, u32[]{:S(2)}) copy-start(bf16[1024,128]{1,0:T(8,128)(2,1)} %param.3) | copy-start | bytes 786436
  1365.9 311.9 %copy-start.1 = (f32[32,128]{1,0:T(8,128)S(1)}, f32[32,128]{1,0:T(8,128)}, u32[]{:S(2)}) copy-start(f32[32,128]{1,0:T(8,128)} %reduce-scatter.2.cloned.1.call-done) | copy-start | bytes 49156
Sparse Core Ops, SparseCore 0:
  100.9 1264.9 reduce-scatter.1
where the time goes:
time: 1690 us
  waiting for transfers between devices  1270 us (75%)
  blocking collectives  395 us (23%)
    reduce_scatter x1, waiting for transfers between devices, body(): lax.psum_scatter(blocks, ('state', 'snap'), scatter_dimension=0, tiled=True)  1270 us
    psum x1, blocking collectives, body(): energy = lax.psum(partial_energy, ('state', 'snap'))  309 us
    all_to_all x1, blocking collectives, body(): lax.all_to_all(snapshots, 'snap', split_axis=1, concat_axis=0, tiled=True)  86.2 us
  transfers between devices with their start and end apart: 1, of which 1 were waited for; matrix products, arithmetic and copies ran while one was open for 0% of the time, Pallas kernels for 0%

commit v1 on v0

v1 whole, which is shorter than its diff:
```python
import jax
import jax.numpy as jnp
from jax import lax
from jax.sharding import Mesh, PartitionSpec as P

NS = 1024
PLANE = ("zlo", "y", "x")
SNAP = ("x", "zhi", "core")
STATE = ("zlo", "y")


def body(snapshots, coefficients):
    width, count = snapshots.shape
    parts = lax.axis_size(SNAP)
    stripes = lax.axis_size(STATE)
    nx, nz, nc = (lax.axis_size(a) for a in SNAP)
    group = stripes * nx
    col = NS // stripes
    all_rows = count * stripes
    core = lax.axis_index("core")
    row_block = lax.all_to_all(snapshots, SNAP, split_axis=1, concat_axis=0, tiled=True)
    raw = lax.dot_general(
        row_block, coefficients, (((0,), (0,)), ((), ())), preferred_element_type=jnp.float32
    )
    energy = jnp.sum(raw * raw, axis=0)
    left = row_block.reshape(nx, nz, nc, width, -1)
    right = row_block.reshape(stripes, col, -1)
    gram = jnp.einsum("xzkrn,scn->ksxzrc", left, right, preferred_element_type=jnp.float32)
    gram = gram.reshape(nc, group, nz * width, col)
    mine = lax.dynamic_index_in_dim(gram, core, 0, keepdims=False)
    other = lax.dynamic_index_in_dim(gram, 1 - core, 0, keepdims=False)
    swap = [(i, 1 - i) for i in range(nc)]
    got = lax.ppermute(other, "core", swap)
    energy = energy + lax.ppermute(energy, "core", swap)
    half = mine + got
    tail = jnp.broadcast_to(energy[None, None, :], (group, 8, col))
    sent = jnp.concatenate([half, tail], axis=1)
    plane = jnp.sum(lax.all_to_all(sent, PLANE, 0, 0, tiled=True), axis=0)
    quarter = plane[: nz * width].reshape(nz, width, col)
    tail = jnp.broadcast_to(plane[None, nz * width :], (nz, 8, col))
    sent = jnp.concatenate([quarter, tail], axis=1)
    total = jnp.sum(lax.all_to_all(sent, "zhi", 0, 0, tiled=True), axis=0)
    gram = total[:width] / all_rows
    modes = raw * lax.rsqrt(total[width] / all_rows + 1e-06)
    return (gram, modes)


def solution(mesh):
    fine = Mesh(mesh.devices.reshape(2, 4, 4, 4, 2), ("zlo", "y", "x", "zhi", "core"))
    return jax.shard_map(
        body,
        mesh=fine,
        in_specs=(P(SNAP, STATE), P()),
        out_specs=(P(SNAP, STATE), P(STATE + SNAP, None)),
        check_vma=False,
    )
```

time: 1690 us -> 153 us (0.09)
  waiting for transfers between devices: 1270 us -> 73.4 us
  blocking collectives: 395 us -> 48 us
    reduce_scatter x1 -> x0, waiting for transfers between devices: 1270 us -> none  [body(): lax.psum_scatter(blocks, ('state', 'snap'), scatter_dimension=0, tiled=True)]
    psum x1 -> x0, blocking collectives: 309 us -> none  [body(): energy = lax.psum(partial_energy, ('state', 'snap'))]
    all_to_all x0 -> x1, waiting for transfers between devices: none -> 71.2 us  [body(): lax.all_to_all(snapshots, SNAP, split_axis=1, concat_axis=0, tiled=True)]
    all_to_all x1 -> x2, blocking collectives: 86.2 us -> 48 us  [the longest x1 38.7 us: body(): plane = jnp.sum(lax.all_to_all(sent, PLANE, 0, 0, tiled=True), axis=0)]
  transfers between devices with their start and end apart: 1 -> 3, of which waited for: 1 -> 3; matrix products, arithmetic and copies ran while one was open for 0% -> 1% of each run, Pallas kernels for 0% -> 0%
where the time goes in v1:
time: 153 us; the launch traced here: 152 us
  waiting for transfers between devices  73.4 us (48%)
  blocking collectives  48 us (31%)
  starting transfers between devices  14.1 us (9%)
  local copies, waits for them, and re-layouts  6.3 us (4%)
  matrix products  5.34 us (3%)
  other arithmetic  4.33 us (3%)
    all_to_all x1, waiting for transfers between devices, body(): lax.all_to_all(snapshots, SNAP, split_axis=1, concat_axis=0, tiled=True)  71.2 us
    all_to_all x1, blocking collectives, body(): plane = jnp.sum(lax.all_to_all(sent, PLANE, 0, 0, tiled=True), axis=0)  38.7 us
    all_to_all x1, starting transfers between devices, body(): lax.all_to_all(snapshots, SNAP, split_axis=1, concat_axis=0, tiled=True)  12.6 us
    all_to_all x1, blocking collectives, body(): total = jnp.sum(lax.all_to_all(sent, 'zhi', 0, 0, tiled=True), axis=0)  9.35 us
    all_to_all x1, local copies, waits for them, and re-layouts, body(): lax.all_to_all(snapshots, SNAP, split_axis=1, concat_axis=0, tiled=True)  4.02 us
    dot_general x1, matrix products, body(): jnp.einsum('xzkrn,scn->ksxzrc', left, right, preferred_element_type=jnp.f...  3.44 us
  transfers between devices with their start and end apart: 3, of which 3 were waited for; matrix products, arithmetic and copies ran while one was open for 1% of the time, Pallas kernels for 0%

profile of v1, /device:TPU:1, one launch (start us, length us, event | category | flops | bytes accessed | tf_op | source)
XLA Modules:
  0.0 152.2 jit_solution(11971864560652370170)
XLA Ops:
  0.6 0.0 copy-start
  0.6 4.0 %copy.12 = bf16[4,32,8,1536]{3,2,0,1:T(8,128)(2,1)} copy(bf16[4,32,8,1536]{3,2,1,0:T(8,128)(2,1)} %bitcast.37) | data formatting | bytes 6291456 | tf_op jit(solution)/shard_map/all_to_all | solution.py:21
  4.7 12.6 %all-to-all-start = ((bf16[32,32,1536]{2,0,1:T(8,128)(2,1)}), bf16[32,32,1536]{2,0,1:T(8,128)(2,1)S(1)}, u32[]{:S(2)}, u32[]{:S(2)}) async-start(bf16[32,32,1536]{2,0,1:T(8,128)(2,1)} %bitcast.36), calls=%async_computation | async-start | bytes 6291456 | tf_op jit(solution)/shard_map/all_to_all | solution.py:21
  17.3 71.2 %all-to-all-done = bf16[32,32,1536]{2,0,1:T(8,128)(2,1)S(1)} async-done(((bf16[32,32,1536]{2,0,1:T(8,128)(2,1)}), bf16[32,32,1536]{2,0,1:T(8,128)(2,1)S(1)}, u32[]{:S(2)}, u32[]{:S(2)}) %all-to-all-start) | async-done | bytes 3145760 | tf_op jit(solution)/shard_map/all_to_all | solution.py:21
  88.4 3.4 %convolution_bitcast_fusion = f32[2,8,4,4,32,128]{5,4,0,3,2,1:T(8,128)S(1)} fusion(bf16[8,128,1536,1,1,1]{2,1,5,4,3,0:T(8,128)(2,1)S(1)} %bitcast.31, bf16[4,4,2,32,1536,1]{4,3,2,1,0,5:T(8,128)(2,1)S(1)} %bitcast.32), kind=kOutput, calls=%fused_computation.2 | convolution fusion | flops 3221225472 | bytes 10485760 | tf_op jit(solution)/shard_map/xzkrn,scn->ksxzrc/dot_general | solution.py:28
  91.9 0.6 copy.8
  92.5 0.0 copy-start.1
  92.5 1.6 %dynamic-slice_bitcast_fusion = f32[32,128,128]{2,1,0:T(8,128)} fusion(f32[2,32,128,128]{3,2,1,0:T(8,128)S(1)} %bitcast.34, s32[]{:T(128)S(6)} %select_n.8), kind=kLoop, calls=%fused_computation.4 | loop fusion | bytes 4194308 | tf_op jit(solution)/shard_map/jit(dynamic_index_in_dim)/squeeze | solution.py:31
  94.1 1.5 collective-permute-start
  95.6 0.0 copy-done
  95.6 1.9 %multiply_reduce_fusion = (f32[128]{0:T(128)S(1)}, f32[1536,128]{1,0:T(8,128)}) fusion(bf16[1024,1536]{1,0:T(8,128)(2,1)S(1)} %bitcast.33, bf16[1024,128]{1,0:T(8,128)(2,1)S(1)} %copy-done), kind=kOutput, calls=%fused_computation.5 | convolution fusion | flops 403046272 | bytes 4194816 | tf_op jit(solution)/shard_map/dot_general | solution.py:22
  97.5 0.0 copy-done.1
  97.5 0.0 collective-permute-start.1
  97.5 1.9 %collective-permute-done.1 = f32[128]{0:T(128)S(1)} collective-permute-done((f32[128]{0:T(128)S(1)}, f32[128]{0:T(128)S(1)}, u32[]{:S(2)}, u32[]{:S(2)}) %collective-permute-start.1) | collective-permute-done | bytes 544 | tf_op jit(solution)/shard_map/ppermute | solution.py:34
  99.4 0.3 collective-permute-done
  99.7 2.5 %bitcast_add_fusion = f32[32,128,128]{2,1,0:T(8,128)S(1)} fusion(f32[32,128,128]{2,1,0:T(8,128)} %collective-permute-done, f32[2,32,128,128]{3,2,1,0:T(8,128)} %bitcast.35, s32[]{:T(128)S(6)} %select_n.7), kind=kLoop, calls=%fused_computation.3 | loop fusion | flops 524288 | bytes 6291460 | tf_op jit(solution)/shard_map/add | solution.py:35
  102.2 0.2 pad_maximum_fusion
  102.4 0.0 copy-start.2
  102.4 38.7 %all_to_all.29 = f32[32,136,128]{2,1,0:T(8,128)S(1)} all-to-all(f32[32,136,128]{2,1,0:T(8,128)S(1)} %pad_maximum_fusion), channel_id=1, replica_groups=mesh['zlo'=2,'y'=4,'x'=4,'zhi'=4,'core'=2] {'zlo','y','x'}, dimensions={0} | all-to-all | bytes 4456448 | tf_op jit(solution)/shard_map/all_to_all | solution.py:38
  141.1 0.1 reduce_sum.28
  141.3 9.3 %all_to_all.30 = f32[4,40,128]{2,1,0:T(8,128)S(1)} all-to-all(f32[4,40,128]{2,1,0:T(8,128)S(1)} %pad_maximum_fusion.1), channel_id=1, replica_groups=mesh['zlo'=2,'y'=4,'x'=4,'zhi'=4,'core'=2] {'zhi'}, dimensions={0} | all-to-all | bytes 163840 | tf_op jit(solution)/shard_map/all_to_all | solution.py:42
  150.6 0.6 slice_multiply_fusion
  151.2 0.0 copy-done.2
  151.2 0.9 broadcast_multiply_fusion
  (8 shorter events, 0.1 us)
Async XLA Ops:
  0.6 95.0 %copy-start = (bf16[1024,128]{1,0:T(8,128)(2,1)S(1)}, bf16[1024,128]{1,0:T(8,128)(2,1)}, u32[]{:S(2)}) copy-start(bf16[1024,128]{1,0:T(8,128)(2,1)} %param.3) | copy-start | bytes 786436
  4.7 83.8 %all-to-all-start = ((bf16[32,32,1536]{2,0,1:T(8,128)(2,1)}), bf16[32,32,1536]{2,0,1:T(8,128)(2,1)S(1)}, u32[]{:S(2)}, u32[]{:S(2)}) async-start(bf16[32,32,1536]{2,0,1:T(8,128)(2,1)} %bitcast.36), calls=%async_computation | async-start | bytes 6291456 | tf_op jit(solution)/shard_map/all_to_all | solution.py:21
  92.5 5.0 %copy-start.1 = (f32[2,8,4,4,32,128]{5,4,3,2,1,0:T(8,128)}, f32[2,8,4,4,32,128]{5,4,3,2,1,0:T(8,128)S(1)}, u32[]{:S(2)}) copy-start(f32[2,8,4,4,32,128]{5,4,3,2,1,0:T(8,128)S(1)} %copy.8) | copy-start | bytes 12582916
  94.1 5.6 %collective-permute-start = (f32[32,128,128]{2,1,0:T(8,128)}, f32[32,128,128]{2,1,0:T(8,128)}, u32[]{:S(2)}, u32[]{:S(2)}) collective-permute-start(f32[32,128,128]{2,1,0:T(8,128)} %dynamic-slice_bitcast_fusion), channel_id=1, source_target_pairs={{0,1},{1,0},{2,3},{3,2},{4,5},{5,4},{6,7},{7,6},{8,9},{9,8},{10,11... | collective-permute-start | bytes 6291464 | tf_op jit(solution)/shard_map/ppermute | solution.py:33
  97.5 1.9 %collective-permute-start.1 = (f32[128]{0:T(128)S(1)}, f32[128]{0:T(128)S(1)}, u32[]{:S(2)}, u32[]{:S(2)}) collective-permute-start(f32[128]{0:T(128)S(1)} %get-tuple-element.2), channel_id=1, source_target_pairs={{0,1},{1,0},{2,3},{3,2},{4,5},{5,4},{6,7},{7,6},{8,9},{9,8},{10,11... | collective-permute-start | bytes 1544 | tf_op jit(solution)/shard_map/ppermute | solution.py:34
  102.4 48.8 %copy-start.2 = (f32[1536,128]{1,0:T(8,128)S(1)}, f32[1536,128]{1,0:T(8,128)}, u32[]{:S(2)}) copy-start(f32[1536,128]{1,0:T(8,128)} %get-tuple-element.3) | copy-start | bytes 2359300

commit v2 on v1

v2 whole, which is shorter than its diff:
```python
import functools

import jax
import jax.numpy as jnp
from jax import lax
from jax.experimental import pallas as pl
from jax.experimental.pallas import tpu as pltpu
from jax.sharding import Mesh, PartitionSpec as P

ALL = ("zlo", "y", "x", "zhi", "core")
PLANE = ("zlo", "y", "x")
SNAP = ("x", "zhi", "core")
STATE = ("zlo", "y")
B = 128
NB = 8
W = 32
HALF = 40
CHUNK = 2 * HALF
PAIR = 2 * B
F32 = jnp.float32


def block(a, s):
    return s * (s + 1) // 2 + a


BLOCKS = NB * (NB + 1) // 2


def gram_kernel(core_ref, rows_ref, coef_ref, mine_ref, other_ref, raw_ref, tile_ref):
    core = core_ref[0]
    raw_t = lax.dot_general(
        coef_ref[...], rows_ref[...], (((0,), (0,)), ((), ())), preferred_element_type=F32
    )
    raw = raw_t.T
    raw_ref[...] = raw
    energy = jnp.broadcast_to(jnp.sum(raw * raw, axis=0, keepdims=True), (W, B))
    mine_ref[pl.ds(BLOCKS, W, stride=CHUNK), :] = energy
    other_ref[pl.ds(BLOCKS, W, stride=CHUNK), :] = energy
    for sp in range(NB // 2):
        depth = (sp + 1) * PAIR
        tile_ref[:depth, :] = lax.dot_general(
            rows_ref[:depth, :],
            rows_ref[sp * PAIR : (sp + 1) * PAIR, :],
            (((1,), (1,)), ((), ())),
            preferred_element_type=F32,
        )
        for t in range(2):
            s = 2 * sp + t
            for a in range(s + 1):
                for slot in range(2):
                    top = a * B + slot * 2 * W
                    row = slot * HALF + block(a, s)
                    for out_ref, c in ((mine_ref, core), (other_ref, 1 - core)):
                        out_ref[pl.ds(row, W, stride=CHUNK), :] = tile_ref[
                            pl.ds(pl.multiple_of(top + c * W, W), W), t * B : (t + 1) * B
                        ]


def spread_kernel(core_ref, got_ref, out_ref, direct_ref, turned_ref):
    core = core_ref[0]
    total = got_ref[0]
    for i in range(1, W):
        total = total + got_ref[i]
    u = (total[:HALF], total[HALF:])
    energy = total[BLOCKS : BLOCKS + 1]
    lane = lax.broadcasted_iota(jnp.int32, (HALF, B), 1)
    part = jnp.where(core == 0, pltpu.roll(energy, B // 2, 1), energy)
    part = jnp.broadcast_to(part, (HALF, B))
    whole = jnp.broadcast_to(energy, (HALF, B))
    for q in range(B // W):
        direct_ref[q] = jnp.where(core == q % 2, u[q // 2], whole)
        first = u[0] if q == 0 else pltpu.roll(u[0], B - W * q, 1)
        second = u[1] if q == 1 else pltpu.roll(u[1], (W - W * q) % B, 1)
        turned_ref[q] = jnp.where(lane < W, first, jnp.where(lane < 2 * W, second, part))
    for s in range(NB):
        for a in range(NB):
            for q in range(B // W):
                dst = s * W + a * (B // W) + q
                if a <= s:
                    row = direct_ref[q, pl.ds(block(a, s), 1), :]
                else:
                    row = turned_ref[q, pl.ds(block(s, a), 1), :]
                out_ref[pl.ds(dst, 1), :] = row


def finish_kernel(all_rows, nz, flag_ref, got_ref, raw_ref, gram_ref, modes_ref):
    core, straight = flag_ref[0], flag_ref[1]
    sums = []
    for c in range(2):
        total = got_ref[pl.ds(c, W, stride=2 * nz), :]
        for z in range(1, nz):
            total = total + got_ref[pl.ds(2 * z + c, W, stride=2 * nz), :]
        sums.append(total)
    direct = jnp.where(core == 0, sums[0], sums[1])
    whole = jnp.where(core == 0, sums[1], sums[0])[:1]
    turned = jnp.concatenate([sums[0], sums[1], sums[0], sums[1]], axis=0).T
    lane = lax.broadcasted_iota(jnp.int32, (W, B), 1)
    turned = jnp.where(lane < B // 2, turned[:W], turned[W : 2 * W])
    halves = jnp.where(lane[:1] < B // 2, pltpu.roll(sums[0][:1], B // 2, 1), sums[1][:1])
    gram_ref[...] = jnp.where(straight == 1, direct, turned) / all_rows
    energy = jnp.where(straight == 1, whole, halves)
    modes_ref[...] = raw_ref[...] * lax.rsqrt(energy / all_rows + 1e-06)


VMEM = pl.BlockSpec(memory_space=pltpu.VMEM)
SMEM = pl.BlockSpec(memory_space=pltpu.SMEM)


def call(kernel, ins, outs, scratch, flops, moved):
    return pl.pallas_call(
        kernel,
        in_specs=[SMEM] + [VMEM] * ins,
        out_specs=tuple(VMEM for _ in outs),
        out_shape=tuple(jax.ShapeDtypeStruct(shape, F32) for shape in outs),
        scratch_shapes=[pltpu.VMEM(shape, F32) for shape in scratch],
        compiler_params=pltpu.CompilerParams(vmem_limit_bytes=40 << 20),
        cost_estimate=pl.CostEstimate(flops=flops, bytes_accessed=moved, transcendentals=0),
    )


def body(snapshots, coefficients):
    count = snapshots.shape[1]
    nz, nc = lax.axis_size("zhi"), lax.axis_size("core")
    all_rows = count * lax.axis_size(STATE)
    devices = lax.axis_size(ALL)
    core = lax.axis_index("core").astype(jnp.int32)
    own_row = lax.axis_index(SNAP) * W // B
    straight = (own_row <= lax.axis_index(STATE)).astype(jnp.int32)
    rows = lax.all_to_all(snapshots, SNAP, split_axis=1, concat_axis=0, tiled=True)
    n = rows.shape[1]
    ns = rows.shape[0]
    mine, other, raw = call(
        gram_kernel,
        2,
        [(W * CHUNK, B), (W * CHUNK, B), (n, B)],
        [(ns, PAIR)],
        2 * ns * n * (5 * ns // 8 + B),
        2 * ns * n + 8 * W * CHUNK * B + 4 * n * B,
    )(core[None], rows, coefficients)
    swap = [(i, 1 - i) for i in range(nc)]
    half = mine + lax.ppermute(other, "core", swap)
    got = lax.all_to_all(half.reshape(W, CHUNK, B), PLANE, 0, 0, tiled=True)
    (spread,) = call(
        spread_kernel, 1, [(devices, B)], [(B // W, HALF, B)] * 2, W * CHUNK * B, 4 * W * CHUNK * B
    )(core[None], got)
    got = lax.all_to_all(spread.reshape(devices, 1, B), ALL, 0, 0, tiled=True)
    gram, modes = call(
        functools.partial(finish_kernel, all_rows, nz),
        2,
        [(W, B), (n, B)],
        [],
        n * B,
        8 * n * B,
    )(jnp.stack([core, straight]), got.reshape(devices, B), raw)
    return (gram, modes)


def solution(mesh):
    fine = Mesh(mesh.devices.reshape(2, 4, 4, 4, 2), ALL)
    return jax.shard_map(
        body,
        mesh=fine,
        in_specs=(P(SNAP, STATE), P()),
        out_specs=(P(SNAP, STATE), P(STATE + SNAP, None)),
        check_vma=False,
    )
```

time: 153 us -> 148 us (0.967)
  blocking collectives: 48 us -> 28.6 us
  waiting for transfers between devices: 73.4 us -> 86.7 us
  starting transfers between devices: 14.1 us -> 20.9 us
  Pallas kernels: 0 us -> 6.29 us
  matrix products: 5.34 us -> 0 us
  other arithmetic: 4.33 us -> 0.25 us
  local copies, waits for them, and re-layouts: 6.3 us -> 3.96 us
    all_to_all x2 -> x1, blocking collectives: 48 us -> 28.6 us  [body(): got = lax.all_to_all(half.reshape(W, CHUNK, B), PLANE, 0, 0, tiled=True)]
    all_to_all x0 -> x1, waiting for transfers between devices: none -> 12.9 us  [body(): got = lax.all_to_all(spread.reshape(devices, 1, B), ALL, 0, 0, tiled=True)]
    all_to_all x0 -> x1, starting transfers between devices: none -> 6.64 us  [body(): got = lax.all_to_all(spread.reshape(devices, 1, B), ALL, 0, 0, tiled=True)]
    pallas_call x0 -> x3, Pallas kernels: none -> 6.29 us  [the longest x1 3.88 us: body(): call(gram_kernel, 2, [(W * CHUNK, B), (W * CHUNK, B), (n, B)], [(ns, PAIR...]
    dot_general x2 -> x0, matrix products: 5.34 us -> none  [the longest x1 3.44 us: body(): jnp.einsum('xzkrn,scn->ksxzrc', left, right, preferred_element_type=jnp.f...]
    add x2 -> x1, other arithmetic: 2.48 us -> 0.17 us  [body(): half = mine + lax.ppermute(other, 'core', swap)]
    squeeze x1 -> x0, local copies, waits for them, and re-layouts: 1.6 us -> none  [body(): other = lax.dynamic_index_in_dim(gram, 1 - core, 0, keepdims=False)]
  transfers between devices with their start and end apart: 3 -> 3, of which waited for: 3 -> 3; matrix products, arithmetic and copies ran while one was open for 1% -> 0% of each run, Pallas kernels for 0% -> 0%
where the time goes in v2:
time: 148 us; the launch traced here: 147 us
  waiting for transfers between devices  86.7 us (59%)
  blocking collectives  28.6 us (19%)
  starting transfers between devices  20.9 us (14%)
  Pallas kernels  6.29 us (4%)
  local copies, waits for them, and re-layouts  3.96 us (3%)
    all_to_all x1, waiting for transfers between devices, body(): lax.all_to_all(snapshots, SNAP, split_axis=1, concat_axis=0, tiled=True)  71.2 us
    all_to_all x1, blocking collectives, body(): got = lax.all_to_all(half.reshape(W, CHUNK, B), PLANE, 0, 0, tiled=True)  28.6 us
    all_to_all x1, waiting for transfers between devices, body(): got = lax.all_to_all(spread.reshape(devices, 1, B), ALL, 0, 0, tiled=True)  12.9 us
    all_to_all x1, starting transfers between devices, body(): lax.all_to_all(snapshots, SNAP, split_axis=1, concat_axis=0, tiled=True)  12.7 us
    all_to_all x1, starting transfers between devices, body(): got = lax.all_to_all(spread.reshape(devices, 1, B), ALL, 0, 0, tiled=True)  6.64 us
    all_to_all x1, local copies, waits for them, and re-layouts, body(): lax.all_to_all(snapshots, SNAP, split_axis=1, concat_axis=0, tiled=True)  3.95 us
    pallas_call x1, Pallas kernels, body(): call(gram_kernel, 2, [(W * CHUNK, B), (W * CHUNK, B), (n, B)], [(ns, PAIR...  3.88 us
  transfers between devices with their start and end apart: 3, of which 3 were waited for; matrix products, arithmetic and copies ran while one was open for 0% of the time, Pallas kernels for 0%

profile of v2, /device:TPU:1, one launch (start us, length us, event | category | flops | bytes accessed | tf_op | source)
XLA Modules:
  0.0 147.5 jit_solution(9202790178090294319)
XLA Ops:
  0.6 4.0 %copy.9 = bf16[4,32,8,1536]{3,2,0,1:T(8,128)(2,1)} copy(bf16[4,32,8,1536]{3,2,1,0:T(8,128)(2,1)} %bitcast.18) | data formatting | bytes 6291456 | tf_op jit(solution)/shard_map/all_to_all | solution.py:130
  4.6 0.0 copy-start.2
  4.6 12.7 %all-to-all-start = ((bf16[32,32,1536]{2,0,1:T(8,128)(2,1)}), bf16[32,32,1536]{2,0,1:T(8,128)(2,1)S(1)}, u32[]{:S(2)}, u32[]{:S(2)}) async-start(bf16[32,32,1536]{2,0,1:T(8,128)(2,1)} %bitcast.16), calls=%async_computation | async-start | bytes 6291456 | tf_op jit(solution)/shard_map/all_to_all | solution.py:130
  17.3 71.2 %all-to-all-done = bf16[32,32,1536]{2,0,1:T(8,128)(2,1)S(1)} async-done(((bf16[32,32,1536]{2,0,1:T(8,128)(2,1)}), bf16[32,32,1536]{2,0,1:T(8,128)(2,1)S(1)}, u32[]{:S(2)}, u32[]{:S(2)}) %all-to-all-start) | async-done | bytes 3145760 | tf_op jit(solution)/shard_map/all_to_all | solution.py:130
  88.5 0.0 copy-done.2
  88.5 3.9 %shard_map.41 = (f32[2560,128]{1,0:T(8,128)S(1)}, f32[2560,128]{1,0:T(8,128)S(1)}, f32[1536,128]{1,0:T(8,128)S(1)}) custom-call(s32[1]{0:T(128)} %bitcast.core_ref, bf16[1024,1536]{1,0:T(8,128)(2,1)S(1)} %bitcast.14, bf16[1024,128]{1,0:T(8,128)(2,1)S(1)} %copy-done.2), custom_call_target="tpu_custom_call" | custom-call | flops 2415919104 | bytes 6553600 | tf_op jit(solution)/shard_map/pallas_call | solution.py:133
  92.4 0.0 copy-start
  92.4 1.6 %collective-permute-start = (f32[2560,128]{1,0:T(8,128)S(1)}, f32[2560,128]{1,0:T(8,128)S(1)}, u32[]{:S(2)}, u32[]{:S(2)}) collective-permute-start(f32[2560,128]{1,0:T(8,128)S(1)} %get-tuple-element.6), channel_id=1, source_target_pairs={{0,1},{1,0},{2,3},{3,2},{4,5},{5,4},{6,7},{7,6},{8,9},{9,8},{10,11... | collective-permute-start | bytes 3932168 | tf_op jit(solution)/shard_map/ppermute | solution.py:142
  94.0 2.7 %collective-permute-done = f32[2560,128]{1,0:T(8,128)S(1)} collective-permute-done((f32[2560,128]{1,0:T(8,128)S(1)}, f32[2560,128]{1,0:T(8,128)S(1)}, u32[]{:S(2)}, u32[]{:S(2)}) %collective-permute-start) | collective-permute-done | bytes 1310752 | tf_op jit(solution)/shard_map/ppermute | solution.py:142
  96.6 0.2 add.16
  96.8 0.0 copy-done
  96.8 28.6 %all_to_all.29.got_ref = f32[32,80,128]{2,1,0:T(8,128)S(1)} all-to-all(f32[32,80,128]{2,1,0:T(8,128)S(1)} %bitcast.17), channel_id=1, replica_groups=mesh['zlo'=2,'y'=4,'x'=4,'zhi'=4,'core'=2] {'zlo','y','x'}, dimensions={0} | all-to-all | bytes 2621440 | tf_op jit(solution)/shard_map/all_to_all | solution.py:143
  125.4 0.0 copy-start.1
  125.4 0.9 shard_map.42
  126.3 6.6 %all-to-all-start.2 = ((f32[256,1,128]{2,1,0:T(1,128)}), f32[256,1,128]{2,1,0:T(1,128)S(1)}, u32[]{:S(2)}, u32[]{:S(2)}) async-start(f32[256,1,128]{2,1,0:T(1,128)} %bitcast.6), calls=%async_computation.2 | async-start | bytes 262144 | tf_op jit(solution)/shard_map/all_to_all | solution.py:147
  132.9 0.1 pad_add_fusion.flag_ref
  133.0 12.9 %all-to-all-done.2 = f32[256,1,128]{2,1,0:T(1,128)S(1)} async-done(((f32[256,1,128]{2,1,0:T(1,128)}), f32[256,1,128]{2,1,0:T(1,128)S(1)}, u32[]{:S(2)}, u32[]{:S(2)}) %all-to-all-start.2) | async-done | bytes 131104 | tf_op jit(solution)/shard_map/all_to_all | solution.py:147
  145.9 0.0 copy-done.1
  145.9 1.6 %shard_map.43 = (f32[32,128]{1,0:T(8,128)}, f32[1536,128]{1,0:T(8,128)}) custom-call(s32[2]{0:T(128)S(1)} %pad_add_fusion.flag_ref, f32[256,128]{1,0:T(8,128)S(1)} %bitcast.15, f32[1536,128]{1,0:T(8,128)S(1)} %copy-done.1), custom_call_target="tpu_custom_call" | custom-call | flops 196608 | bytes 1572864 | tf_op jit(solution)/shard_map/pallas_call | solution.py:148
Async XLA Ops:
  4.6 83.9 %copy-start.2 = (bf16[1024,128]{1,0:T(8,128)(2,1)S(1)}, bf16[1024,128]{1,0:T(8,128)(2,1)}, u32[]{:S(2)}) copy-start(bf16[1024,128]{1,0:T(8,128)(2,1)} %coef_ref.1) | copy-start | bytes 786436
  4.6 83.9 %all-to-all-start = ((bf16[32,32,1536]{2,0,1:T(8,128)(2,1)}), bf16[32,32,1536]{2,0,1:T(8,128)(2,1)S(1)}, u32[]{:S(2)}, u32[]{:S(2)}) async-start(bf16[32,32,1536]{2,0,1:T(8,128)(2,1)} %bitcast.16), calls=%async_computation | async-start | bytes 6291456 | tf_op jit(solution)/shard_map/all_to_all | solution.py:130
  92.4 4.4 %copy-start = (f32[1536,128]{1,0:T(8,128)}, f32[1536,128]{1,0:T(8,128)S(1)}, u32[]{:S(2)}) copy-start(f32[1536,128]{1,0:T(8,128)S(1)} %get-tuple-element.7.raw_ref) | copy-start | bytes 2359300
  92.4 4.2 %collective-permute-start = (f32[2560,128]{1,0:T(8,128)S(1)}, f32[2560,128]{1,0:T(8,128)S(1)}, u32[]{:S(2)}, u32[]{:S(2)}) collective-permute-start(f32[2560,128]{1,0:T(8,128)S(1)} %get-tuple-element.6), channel_id=1, source_target_pairs={{0,1},{1,0},{2,3},{3,2},{4,5},{5,4},{6,7},{7,6},{8,9},{9,8},{10,11... | collective-permute-start | bytes 3932168 | tf_op jit(solution)/shard_map/ppermute | solution.py:142
  125.4 20.5 %copy-start.1 = (f32[1536,128]{1,0:T(8,128)S(1)}, f32[1536,128]{1,0:T(8,128)}, u32[]{:S(2)}) copy-start(f32[1536,128]{1,0:T(8,128)} %copy-done) | copy-start | bytes 2359300
  126.3 19.6 %all-to-all-start.2 = ((f32[256,1,128]{2,1,0:T(1,128)}), f32[256,1,128]{2,1,0:T(1,128)S(1)}, u32[]{:S(2)}, u32[]{:S(2)}) async-start(f32[256,1,128]{2,1,0:T(1,128)} %bitcast.6), calls=%async_computation.2 | async-start | bytes 262144 | tf_op jit(solution)/shard_map/all_to_all | solution.py:147

commit v3 on v2

--- a/solution.py
+++ b/solution.py
@@ -27,8 +27,8 @@
 BLOCKS = NB * (NB + 1) // 2
 
 
-def gram_kernel(core_ref, rows_ref, coef_ref, mine_ref, other_ref, raw_ref, tile_ref):
-    core = core_ref[0]
+def gram_kernel(rows_ref, coef_ref, mine_ref, other_ref, raw_ref, tile_ref):
+    core = lax.axis_index("core")
     raw_t = lax.dot_general(
         coef_ref[...], rows_ref[...], (((0,), (0,)), ((), ())), preferred_element_type=F32
     )
@@ -57,8 +57,8 @@
                         ]
 
 
-def spread_kernel(core_ref, got_ref, out_ref, direct_ref, turned_ref):
-    core = core_ref[0]
+def spread_kernel(got_ref, out_ref, direct_ref, turned_ref):
+    core = lax.axis_index("core")
     total = got_ref[0]
     for i in range(1, W):
         total = total + got_ref[i]
@@ -84,8 +84,9 @@
                 out_ref[pl.ds(dst, 1), :] = row
 
 
-def finish_kernel(all_rows, nz, flag_ref, got_ref, raw_ref, gram_ref, modes_ref):
-    core, straight = flag_ref[0], flag_ref[1]
+def finish_kernel(all_rows, nz, got_ref, raw_ref, gram_ref, modes_ref):
+    core = lax.axis_index("core")
+    straight = lax.axis_index(SNAP) // (B // W) <= lax.axis_index(STATE)
     sums = []
     for c in range(2):
         total = got_ref[pl.ds(c, W, stride=2 * nz), :]
@@ -98,52 +99,54 @@
     lane = lax.broadcasted_iota(jnp.int32, (W, B), 1)
     turned = jnp.where(lane < B // 2, turned[:W], turned[W : 2 * W])
     halves = jnp.where(lane[:1] < B // 2, pltpu.roll(sums[0][:1], B // 2, 1), sums[1][:1])
-    gram_ref[...] = jnp.where(straight == 1, direct, turned) / all_rows
-    energy = jnp.where(straight == 1, whole, halves)
+    gram_ref[...] = jnp.where(straight, direct, turned) / all_rows
+    energy = jnp.where(straight, whole, halves)
     modes_ref[...] = raw_ref[...] * lax.rsqrt(energy / all_rows + 1e-06)
 
 
 VMEM = pl.BlockSpec(memory_space=pltpu.VMEM)
-SMEM = pl.BlockSpec(memory_space=pltpu.SMEM)
 
 
 def call(kernel, ins, outs, scratch, flops, moved):
     return pl.pallas_call(
         kernel,
-        in_specs=[SMEM] + [VMEM] * ins,
+        in_specs=[VMEM] * ins,
         out_specs=tuple(VMEM for _ in outs),
         out_shape=tuple(jax.ShapeDtypeStruct(shape, F32) for shape in outs),
-        scratch_shapes=[pltpu.VMEM(shape, F32) for shape in scratch],
+        scratch_shapes=scratch,
         compiler_params=pltpu.CompilerParams(vmem_limit_bytes=40 << 20),
         cost_estimate=pl.CostEstimate(flops=flops, bytes_accessed=moved, transcendentals=0),
     )
 
 
 def body(snapshots, coefficients):
-    count = snapshots.shape[1]
+    width, count = snapshots.shape
     nz, nc = lax.axis_size("zhi"), lax.axis_size("core")
+    parts = lax.axis_size(SNAP)
+    n = count // parts
+    ns = width * parts
     all_rows = count * lax.axis_size(STATE)
     devices = lax.axis_size(ALL)
-    core = lax.axis_index("core").astype(jnp.int32)
-    own_row = lax.axis_index(SNAP) * W // B
-    straight = (own_row <= lax.axis_index(STATE)).astype(jnp.int32)
     rows = lax.all_to_all(snapshots, SNAP, split_axis=1, concat_axis=0, tiled=True)
-    n = rows.shape[1]
-    ns = rows.shape[0]
     mine, other, raw = call(
         gram_kernel,
         2,
         [(W * CHUNK, B), (W * CHUNK, B), (n, B)],
-        [(ns, PAIR)],
+        [pltpu.VMEM((ns, PAIR), F32)],
         2 * ns * n * (5 * ns // 8 + B),
         2 * ns * n + 8 * W * CHUNK * B + 4 * n * B,
-    )(core[None], rows, coefficients)
+    )(rows, coefficients)
     swap = [(i, 1 - i) for i in range(nc)]
     half = mine + lax.ppermute(other, "core", swap)
     got = lax.all_to_all(half.reshape(W, CHUNK, B), PLANE, 0, 0, tiled=True)
     (spread,) = call(
-        spread_kernel, 1, [(devices, B)], [(B // W, HALF, B)] * 2, W * CHUNK * B, 4 * W * CHUNK * B
-    )(core[None], got)
+        spread_kernel,
+        1,
+        [(devices, B)],
+        [pltpu.VMEM((B // W, HALF, B), F32)] * 2,
+        W * CHUNK * B,
+        4 * W * CHUNK * B,
+    )(got)
     got = lax.all_to_all(spread.reshape(devices, 1, B), ALL, 0, 0, tiled=True)
     gram, modes = call(
         functools.partial(finish_kernel, all_rows, nz),
@@ -152,7 +155,7 @@
         [],
         n * B,
         8 * n * B,
-    )(jnp.stack([core, straight]), got.reshape(devices, B), raw)
+    )(got.reshape(devices, B), raw)
     return (gram, modes)
 
 

time: 148 us -> 144 us (0.973)
  blocking collectives: 28.6 us -> 131 us
  waiting for transfers between devices: 86.7 us -> 2.66 us
  starting transfers between devices: 20.9 us -> 1.84 us
  local copies, waits for them, and re-layouts: 3.96 us -> 2.3 us
    all_to_all x0 -> x2, blocking collectives: none -> 106 us  [the longest x1 86.3 us: body(): lax.all_to_all(snapshots, SNAP, split_axis=1, concat_axis=0, tiled=True)]
    all_to_all x2 -> x0, waiting for transfers between devices: 84.1 us -> none  [the longest x1 71.2 us: body(): lax.all_to_all(snapshots, SNAP, split_axis=1, concat_axis=0, tiled=True)]
    all_to_all x2 -> x0, starting transfers between devices: 19.4 us -> none  [the longest x1 12.7 us: body(): lax.all_to_all(snapshots, SNAP, split_axis=1, concat_axis=0, tiled=True)]
    all_to_all x1, blocking collectives: 28.6 us -> 25.5 us  [body(): got = lax.all_to_all(half.reshape(W, CHUNK, B), PLANE, 0, 0, tiled=True)]
    all_to_all x1, local copies, waits for them, and re-layouts: 3.95 us -> 2.3 us  [body(): lax.all_to_all(snapshots, SNAP, split_axis=1, concat_axis=0, tiled=True)]
  transfers between devices with their start and end apart: 3 -> 1, of which waited for: 3 -> 1; matrix products, arithmetic and copies ran while one was open for 0% -> 0% of each run, Pallas kernels for 0% -> 0%
where the time goes in v3:
time: 144 us
  blocking collectives  131 us (91%)
  Pallas kernels  4.96 us (3%)
  waiting for transfers between devices  2.66 us (2%)
  local copies, waits for them, and re-layouts  2.3 us (2%)
  starting transfers between devices  1.84 us (1%)
    all_to_all x1, blocking collectives, body(): lax.all_to_all(snapshots, SNAP, split_axis=1, concat_axis=0, tiled=True)  86.3 us
    all_to_all x1, blocking collectives, body(): got = lax.all_to_all(half.reshape(W, CHUNK, B), PLANE, 0, 0, tiled=True)  25.5 us
    all_to_all x1, blocking collectives, body(): got = lax.all_to_all(spread.reshape(devices, 1, B), ALL, 0, 0, tiled=True)  19.3 us
    pallas_call x1, Pallas kernels, body(): call(gram_kernel, 2, [(W * CHUNK, B), (W * CHUNK, B), (n, B)], [pltpu.VME...  3.75 us
  transfers between devices with their start and end apart: 1, of which 1 were waited for; matrix products, arithmetic and copies ran while one was open for 0% of the time, Pallas kernels for 0%

profile of v3, /device:TPU:1, one launch (start us, length us, event | category | flops | bytes accessed | tf_op | source)
XLA Modules:
  0.0 143.7 jit_solution(18010755772090885482)
XLA Ops:
  0.6 2.3 %copy.9 = bf16[4,32,8,1536]{3,2,0,1:T(8,128)(2,1)S(1)} copy(bf16[4,32,8,1536]{3,2,1,0:T(8,128)(2,1)} %bitcast.17) | data formatting | bytes 6291456 | tf_op jit(solution)/shard_map/all_to_all | solution.py:130
  2.9 0.0 copy-start
  2.9 86.3 %all_to_all.29 = bf16[32,32,1536]{2,0,1:T(8,128)(2,1)S(1)} all-to-all(bf16[32,32,1536]{2,0,1:T(8,128)(2,1)S(1)} %bitcast.15), channel_id=1, replica_groups=mesh['zlo'=2,'y'=4,'x'=4,'zhi'=4,'core'=2] {'x','zhi','core'}, dimensions={1} | all-to-all | bytes 6291456 | tf_op jit(solution)/shard_map/all_to_all | solution.py:130
  89.2 0.0 copy-done
  89.2 3.7 %shard_map.41 = (f32[2560,128]{1,0:T(8,128)S(1)}, f32[2560,128]{1,0:T(8,128)S(1)}, f32[1536,128]{1,0:T(8,128)S(1)}) custom-call(bf16[1024,1536]{1,0:T(8,128)(2,1)S(1)} %bitcast.12, bf16[1024,128]{1,0:T(8,128)(2,1)S(1)} %copy-done), custom_call_target="tpu_custom_call" | custom-call | flops 2415919104 | bytes 6553600 | tf_op jit(solution)/shard_map/pallas_call | solution.py:131
  93.0 1.8 %collective-permute-start = (f32[2560,128]{1,0:T(8,128)S(1)}, f32[2560,128]{1,0:T(8,128)S(1)}, u32[]{:S(2)}, u32[]{:S(2)}) collective-permute-start(f32[2560,128]{1,0:T(8,128)S(1)} %get-tuple-element.6), channel_id=1, source_target_pairs={{0,1},{1,0},{2,3},{3,2},{4,5},{5,4},{6,7},{7,6},{8,9},{9,8},{10,11... | collective-permute-start | bytes 3932168 | tf_op jit(solution)/shard_map/ppermute | solution.py:140
  94.8 2.7 %collective-permute-done = f32[2560,128]{1,0:T(8,128)S(1)} collective-permute-done((f32[2560,128]{1,0:T(8,128)S(1)}, f32[2560,128]{1,0:T(8,128)S(1)}, u32[]{:S(2)}, u32[]{:S(2)}) %collective-permute-start) | collective-permute-done | bytes 1310752 | tf_op jit(solution)/shard_map/ppermute | solution.py:140
  97.5 0.1 add.3
  97.6 25.5 %all_to_all.30.got_ref = f32[32,80,128]{2,1,0:T(8,128)S(1)} all-to-all(f32[32,80,128]{2,1,0:T(8,128)S(1)} %bitcast.16), channel_id=1, replica_groups=mesh['zlo'=2,'y'=4,'x'=4,'zhi'=4,'core'=2] {'zlo','y','x'}, dimensions={0} | all-to-all | bytes 2621440 | tf_op jit(solution)/shard_map/all_to_all | solution.py:141
  123.1 0.2 shard_map.42
  123.3 19.3 %all_to_all.31 = f32[256,1,128]{2,1,0:T(1,128)S(1)} all-to-all(f32[256,1,128]{2,1,0:T(1,128)S(1)} %bitcast.14), channel_id=1, replica_groups=mesh['zlo'=2,'y'=4,'x'=4,'zhi'=4,'core'=2] {'zlo','y','x','zhi','core'}, dimensions={0} | all-to-all | bytes 262144 | tf_op jit(solution)/shard_map/all_to_all | solution.py:150
  142.7 1.0 shard_map.43
Async XLA Ops:
  2.9 86.3 %copy-start = (bf16[1024,128]{1,0:T(8,128)(2,1)S(1)}, bf16[1024,128]{1,0:T(8,128)(2,1)}, u32[]{:S(2)}) copy-start(bf16[1024,128]{1,0:T(8,128)(2,1)} %coef_ref.1) | copy-start | bytes 786436
  93.0 4.5 %collective-permute-start = (f32[2560,128]{1,0:T(8,128)S(1)}, f32[2560,128]{1,0:T(8,128)S(1)}, u32[]{:S(2)}, u32[]{:S(2)}) collective-permute-start(f32[2560,128]{1,0:T(8,128)S(1)} %get-tuple-element.6), channel_id=1, source_target_pairs={{0,1},{1,0},{2,3},{3,2},{4,5},{5,4},{6,7},{7,6},{8,9},{9,8},{10,11... | collective-permute-start | bytes 3932168 | tf_op jit(solution)/shard_map/ppermute | solution.py:140

commit v4 on v3

--- a/solution.py
+++ b/solution.py
@@ -8,14 +8,15 @@
 from jax.sharding import Mesh, PartitionSpec as P
 
 ALL = ("zlo", "y", "x", "zhi", "core")
-PLANE = ("zlo", "y", "x")
+PLANE = ("x", "y", "zlo")
+SPREAD = PLANE + ("zhi", "core")
 SNAP = ("x", "zhi", "core")
 STATE = ("zlo", "y")
 B = 128
 NB = 8
 W = 32
-HALF = 40
-CHUNK = 2 * HALF
+BLOCKS = NB * (NB + 1) // 2
+CHUNK = 2 * BLOCKS
 PAIR = 2 * B
 F32 = jnp.float32
 
@@ -24,7 +25,14 @@
     return s * (s + 1) // 2 + a
 
 
-BLOCKS = NB * (NB + 1) // 2
+def target(s, a, q):
+    p = a * (B // W) + q
+    x, zhi, core = p // 8, p // 2 % 4, p % 2
+    return (((x * 4 + s % 4) * 2 + s // 4) * 4 + zhi) * 2 + core
+
+
+def low(shape):
+    return lax.broadcasted_iota(jnp.int32, shape, 1) < B // 2
 
 
 def gram_kernel(rows_ref, coef_ref, mine_ref, other_ref, raw_ref, tile_ref):
@@ -34,9 +42,8 @@
     )
     raw = raw_t.T
     raw_ref[...] = raw
-    energy = jnp.broadcast_to(jnp.sum(raw * raw, axis=0, keepdims=True), (W, B))
-    mine_ref[pl.ds(BLOCKS, W, stride=CHUNK), :] = energy
-    other_ref[pl.ds(BLOCKS, W, stride=CHUNK), :] = energy
+    energy = jnp.sum(raw * raw, axis=0, keepdims=True)
+    energies = [energy, pltpu.roll(energy, B // 2, 1)]
     for sp in range(NB // 2):
         depth = (sp + 1) * PAIR
         tile_ref[:depth, :] = lax.dot_general(
@@ -50,57 +57,72 @@
             for a in range(s + 1):
                 for slot in range(2):
                     top = a * B + slot * 2 * W
-                    row = slot * HALF + block(a, s)
+                    row = slot * BLOCKS + block(a, s)
                     for out_ref, c in ((mine_ref, core), (other_ref, 1 - core)):
-                        out_ref[pl.ds(row, W, stride=CHUNK), :] = tile_ref[
+                        part = tile_ref[
                             pl.ds(pl.multiple_of(top + c * W, W), W), t * B : (t + 1) * B
                         ]
+                        if slot == 1 and a == s < 2:
+                            part = jnp.where(low((W, B)), jnp.broadcast_to(energies[s], (W, B)), part)
+                        out_ref[pl.ds(row, W, stride=CHUNK), :] = part
 
 
-def spread_kernel(got_ref, out_ref, direct_ref, turned_ref):
+def spread_kernel(got_ref, out_ref, direct_ref, turned_ref, mixed_ref):
     core = lax.axis_index("core")
+    chip = lax.axis_index(PLANE)
     total = got_ref[0]
     for i in range(1, W):
         total = total + got_ref[i]
-    u = (total[:HALF], total[HALF:])
-    energy = total[BLOCKS : BLOCKS + 1]
-    lane = lax.broadcasted_iota(jnp.int32, (HALF, B), 1)
-    part = jnp.where(core == 0, pltpu.roll(energy, B // 2, 1), energy)
-    part = jnp.broadcast_to(part, (HALF, B))
-    whole = jnp.broadcast_to(energy, (HALF, B))
+    u = (total[:BLOCKS], total[BLOCKS:])
+    first, second = (u[1][block(s, s) : block(s, s) + 1] for s in range(2))
+    energy = jnp.where(low((1, B)), first, pltpu.roll(second, B // 2, 1))
+    swapped = pltpu.roll(energy, B // 2, 1)
+    shape = (BLOCKS, B)
+    whole = jnp.broadcast_to(energy, shape)
+    by_core = jnp.broadcast_to(jnp.where(core == 0, swapped, energy), shape)
+    by_chip = jnp.broadcast_to(jnp.where(chip < W // 2, swapped, energy), shape)
+    lane = lax.broadcasted_iota(jnp.int32, shape, 1)
     for q in range(B // W):
-        direct_ref[q] = jnp.where(core == q % 2, u[q // 2], whole)
+        own = core == q % 2
+        direct_ref[q] = jnp.where(own, u[q // 2], whole)
         first = u[0] if q == 0 else pltpu.roll(u[0], B - W * q, 1)
         second = u[1] if q == 1 else pltpu.roll(u[1], (W - W * q) % B, 1)
-        turned_ref[q] = jnp.where(lane < W, first, jnp.where(lane < 2 * W, second, part))
+        turned_ref[q] = jnp.where(lane < W, first, jnp.where(lane < 2 * W, second, by_core))
+        mixed_ref[q] = jnp.where(lane < W, first, jnp.where(own, u[1], by_chip))
     for s in range(NB):
         for a in range(NB):
             for q in range(B // W):
-                dst = s * W + a * (B // W) + q
-                if a <= s:
+                if a == s < 2 and q >= 2:
+                    row = mixed_ref[q, pl.ds(block(a, s), 1), :]
+                elif a <= s:
                     row = direct_ref[q, pl.ds(block(a, s), 1), :]
                 else:
                     row = turned_ref[q, pl.ds(block(s, a), 1), :]
-                out_ref[pl.ds(dst, 1), :] = row
+                out_ref[pl.ds(target(s, a, q), 1), :] = row
 
 
 def finish_kernel(all_rows, nz, got_ref, raw_ref, gram_ref, modes_ref):
-    core = lax.axis_index("core")
-    straight = lax.axis_index(SNAP) // (B // W) <= lax.axis_index(STATE)
+    place, stripe = lax.axis_index(SNAP), lax.axis_index(STATE)
+    q, own_row = place % (B // W), place // (B // W)
+    even = q % 2 == 0
+    straight = own_row <= stripe
+    mixed = jnp.logical_and(jnp.logical_and(own_row == stripe, stripe < 2), q >= 2)
     sums = []
     for c in range(2):
         total = got_ref[pl.ds(c, W, stride=2 * nz), :]
         for z in range(1, nz):
             total = total + got_ref[pl.ds(2 * z + c, W, stride=2 * nz), :]
         sums.append(total)
-    direct = jnp.where(core == 0, sums[0], sums[1])
-    whole = jnp.where(core == 0, sums[1], sums[0])[:1]
-    turned = jnp.concatenate([sums[0], sums[1], sums[0], sums[1]], axis=0).T
-    lane = lax.broadcasted_iota(jnp.int32, (W, B), 1)
-    turned = jnp.where(lane < B // 2, turned[:W], turned[W : 2 * W])
-    halves = jnp.where(lane[:1] < B // 2, pltpu.roll(sums[0][:1], B // 2, 1), sums[1][:1])
-    gram_ref[...] = jnp.where(straight, direct, turned) / all_rows
-    energy = jnp.where(straight, whole, halves)
+    direct = jnp.where(even, sums[0], sums[1])
+    spare = jnp.where(even, sums[1], sums[0])
+    flipped = jnp.concatenate([sums[0], sums[1], sums[0], sums[1]], axis=0).T
+    left, one = low((W, B)), low((1, B))
+    turned = jnp.where(left, flipped[:W], flipped[W : 2 * W])
+    both = jnp.where(left, flipped[:W], direct)
+    gram_ref[...] = jnp.where(straight, jnp.where(mixed, both, direct), turned) / all_rows
+    by_core = jnp.where(one, pltpu.roll(sums[0][:1], B // 2, 1), sums[1][:1])
+    by_chip = jnp.where(one, pltpu.roll(spare[:1], B // 2, 1), spare[W // 2 : W // 2 + 1])
+    energy = jnp.where(straight, jnp.where(mixed, by_chip, spare[:1]), by_core)
     modes_ref[...] = raw_ref[...] * lax.rsqrt(energy / all_rows + 1e-06)
 
 
@@ -143,11 +165,11 @@
         spread_kernel,
         1,
         [(devices, B)],
-        [pltpu.VMEM((B // W, HALF, B), F32)] * 2,
+        [pltpu.VMEM((B // W, BLOCKS, B), F32)] * 3,
         W * CHUNK * B,
         4 * W * CHUNK * B,
     )(got)
-    got = lax.all_to_all(spread.reshape(devices, 1, B), ALL, 0, 0, tiled=True)
+    got = lax.all_to_all(spread.reshape(devices, 1, B), SPREAD, 0, 0, tiled=True)
     gram, modes = call(
         functools.partial(finish_kernel, all_rows, nz),
         2,

time: 144 us -> 142 us (0.986)
  no operation moved by 1% of the time
where the time goes in v4:
time: 142 us
  blocking collectives  130 us (92%)
  Pallas kernels  4.61 us (3%)
  waiting for transfers between devices  2.47 us (2%)
  local copies, waits for them, and re-layouts  2.3 us (2%)
  starting transfers between devices  1.83 us (1%)
    all_to_all x1, blocking collectives, body(): lax.all_to_all(snapshots, SNAP, split_axis=1, concat_axis=0, tiled=True)  86.3 us
    all_to_all x1, blocking collectives, body(): got = lax.all_to_all(half.reshape(W, CHUNK, B), PLANE, 0, 0, tiled=True)  24.8 us
    all_to_all x1, blocking collectives, body(): lax.all_to_all(spread.reshape(devices, 1, B), SPREAD, 0, 0, tiled=True)  18.8 us
    pallas_call x1, Pallas kernels, body(): call(gram_kernel, 2, [(W * CHUNK, B), (W * CHUNK, B), (n, B)], [pltpu.VME...  3.34 us
  transfers between devices with their start and end apart: 1, of which 1 were waited for; matrix products, arithmetic and copies ran while one was open for 0% of the time, Pallas kernels for 0%

profile of v4, /device:TPU:1, one launch (start us, length us, event | category | flops | bytes accessed | tf_op | source)
XLA Modules:
  0.0 141.9 jit_solution(15008095477023747918)
XLA Ops:
  0.6 2.3 %copy.9 = bf16[4,32,8,1536]{3,2,0,1:T(8,128)(2,1)S(1)} copy(bf16[4,32,8,1536]{3,2,1,0:T(8,128)(2,1)} %bitcast.17) | data formatting | bytes 6291456 | tf_op jit(solution)/shard_map/all_to_all | solution.py:152
  2.9 0.0 copy-start
  2.9 86.3 %all_to_all.29 = bf16[32,32,1536]{2,0,1:T(8,128)(2,1)S(1)} all-to-all(bf16[32,32,1536]{2,0,1:T(8,128)(2,1)S(1)} %bitcast.15), channel_id=1, replica_groups=mesh['zlo'=2,'y'=4,'x'=4,'zhi'=4,'core'=2] {'x','zhi','core'}, dimensions={1} | all-to-all | bytes 6291456 | tf_op jit(solution)/shard_map/all_to_all | solution.py:152
  89.2 0.0 copy-done
  89.2 3.3 %shard_map.41 = (f32[2304,128]{1,0:T(8,128)S(1)}, f32[2304,128]{1,0:T(8,128)S(1)}, f32[1536,128]{1,0:T(8,128)S(1)}) custom-call(bf16[1024,1536]{1,0:T(8,128)(2,1)S(1)} %bitcast.12, bf16[1024,128]{1,0:T(8,128)(2,1)S(1)} %copy-done), custom_call_target="tpu_custom_call" | custom-call | flops 2415919104 | bytes 6291456 | tf_op jit(solution)/shard_map/pallas_call | solution.py:153
  92.6 1.8 %collective-permute-start = (f32[2304,128]{1,0:T(8,128)S(1)}, f32[2304,128]{1,0:T(8,128)S(1)}, u32[]{:S(2)}, u32[]{:S(2)}) collective-permute-start(f32[2304,128]{1,0:T(8,128)S(1)} %get-tuple-element.6), channel_id=1, source_target_pairs={{0,1},{1,0},{2,3},{3,2},{4,5},{5,4},{6,7},{7,6},{8,9},{9,8},{10,11... | collective-permute-start | bytes 3538952 | tf_op jit(solution)/shard_map/ppermute | solution.py:162
  94.4 2.5 %collective-permute-done = f32[2304,128]{1,0:T(8,128)S(1)} collective-permute-done((f32[2304,128]{1,0:T(8,128)S(1)}, f32[2304,128]{1,0:T(8,128)S(1)}, u32[]{:S(2)}, u32[]{:S(2)}) %collective-permute-start) | collective-permute-done | bytes 1179680 | tf_op jit(solution)/shard_map/ppermute | solution.py:162
  96.9 0.1 add.3
  97.0 24.8 %all_to_all.30.got_ref = f32[32,72,128]{2,1,0:T(8,128)S(1)} all-to-all(f32[32,72,128]{2,1,0:T(8,128)S(1)} %bitcast.16), channel_id=1, replica_groups=mesh['zlo'=2,'y'=4,'x'=4,'zhi'=4,'core'=2] {'x','y','zlo'}, dimensions={0} | all-to-all | bytes 2359296 | tf_op jit(solution)/shard_map/all_to_all | solution.py:163
  121.8 0.2 shard_map.42
  122.0 18.8 %all_to_all.31 = f32[256,1,128]{2,1,0:T(1,128)S(1)} all-to-all(f32[256,1,128]{2,1,0:T(1,128)S(1)} %bitcast.14), channel_id=1, replica_groups=mesh['zlo'=2,'y'=4,'x'=4,'zhi'=4,'core'=2] {'x','y','zlo','zhi','core'}, dimensions={0} | all-to-all | bytes 262144 | tf_op jit(solution)/shard_map/all_to_all | solution.py:172
  140.8 1.0 shard_map.43
Async XLA Ops:
  2.9 86.3 %copy-start = (bf16[1024,128]{1,0:T(8,128)(2,1)S(1)}, bf16[1024,128]{1,0:T(8,128)(2,1)}, u32[]{:S(2)}) copy-start(bf16[1024,128]{1,0:T(8,128)(2,1)} %coef_ref.1) | copy-start | bytes 786436
  92.6 4.3 %collective-permute-start = (f32[2304,128]{1,0:T(8,128)S(1)}, f32[2304,128]{1,0:T(8,128)S(1)}, u32[]{:S(2)}, u32[]{:S(2)}) collective-permute-start(f32[2304,128]{1,0:T(8,128)S(1)} %get-tuple-element.6), channel_id=1, source_target_pairs={{0,1},{1,0},{2,3},{3,2},{4,5},{5,4},{6,7},{7,6},{8,9},{9,8},{10,11... | collective-permute-start | bytes 3538952 | tf_op jit(solution)/shard_map/ppermute | solution.py:162

commit v5 on v4

--- a/solution.py
+++ b/solution.py
@@ -35,15 +35,8 @@
     return lax.broadcasted_iota(jnp.int32, shape, 1) < B // 2
 
 
-def gram_kernel(rows_ref, coef_ref, mine_ref, other_ref, raw_ref, tile_ref):
+def gram_kernel(rows_ref, mine_ref, other_ref, tile_ref):
     core = lax.axis_index("core")
-    raw_t = lax.dot_general(
-        coef_ref[...], rows_ref[...], (((0,), (0,)), ((), ())), preferred_element_type=F32
-    )
-    raw = raw_t.T
-    raw_ref[...] = raw
-    energy = jnp.sum(raw * raw, axis=0, keepdims=True)
-    energies = [energy, pltpu.roll(energy, B // 2, 1)]
     for sp in range(NB // 2):
         depth = (sp + 1) * PAIR
         tile_ref[:depth, :] = lax.dot_general(
@@ -62,9 +55,16 @@
                         part = tile_ref[
                             pl.ds(pl.multiple_of(top + c * W, W), W), t * B : (t + 1) * B
                         ]
-                        if slot == 1 and a == s < 2:
-                            part = jnp.where(low((W, B)), jnp.broadcast_to(energies[s], (W, B)), part)
                         out_ref[pl.ds(row, W, stride=CHUNK), :] = part
+
+
+def raw_kernel(rows_ref, coef_ref, raw_ref, energy_ref):
+    raw_t = lax.dot_general(
+        coef_ref[...], rows_ref[...], (((0,), (0,)), ((), ())), preferred_element_type=F32
+    )
+    raw = raw_t.T
+    raw_ref[...] = raw
+    energy_ref[...] = jnp.sum(raw * raw, axis=0, keepdims=True)
 
 
 def spread_kernel(got_ref, out_ref, direct_ref, turned_ref, mixed_ref):
@@ -150,17 +150,27 @@
     all_rows = count * lax.axis_size(STATE)
     devices = lax.axis_size(ALL)
     rows = lax.all_to_all(snapshots, SNAP, split_axis=1, concat_axis=0, tiled=True)
-    mine, other, raw = call(
+    mine, other = call(
         gram_kernel,
-        2,
-        [(W * CHUNK, B), (W * CHUNK, B), (n, B)],
+        1,
+        [(W * CHUNK, B), (W * CHUNK, B)],
         [pltpu.VMEM((ns, PAIR), F32)],
-        2 * ns * n * (5 * ns // 8 + B),
-        2 * ns * n + 8 * W * CHUNK * B + 4 * n * B,
+        2 * ns * n * 5 * ns // 8,
+        2 * ns * n + 8 * W * CHUNK * B,
+    )(rows)
+    swap = [(i, 1 - i) for i in range(nc)]
+    got = lax.ppermute(other, "core", swap)
+    raw, energy = call(
+        raw_kernel, 2, [(n, B), (1, B)], [], 2 * ns * n * B, 2 * ns * n + 4 * n * B
     )(rows, coefficients)
-    swap = [(i, 1 - i) for i in range(nc)]
-    half = mine + lax.ppermute(other, "core", swap)
-    got = lax.all_to_all(half.reshape(W, CHUNK, B), PLANE, 0, 0, tiled=True)
+    energy = energy + lax.ppermute(energy, "core", swap)
+    place = lax.broadcasted_iota(jnp.int32, (1, CHUNK, B), 1) - BLOCKS
+    left = lax.broadcasted_iota(jnp.int32, (1, CHUNK, B), 2) < B // 2
+    turned = jnp.roll(energy, B // 2, 1)
+    half = (mine + got).reshape(W, CHUNK, B)
+    half = jnp.where(left & (place == block(0, 0)), energy[None], half)
+    half = jnp.where(left & (place == block(1, 1)), turned[None], half)
+    got = lax.all_to_all(half, PLANE, 0, 0, tiled=True)
     (spread,) = call(
         spread_kernel,
         1,

time: 142 us -> 142 us (level)
    pallas_call x1 -> x2, Pallas kernels: 3.34 us -> 3.6 us  [the longest x1 2.86 us: body(): call(gram_kernel, 1, [(W * CHUNK, B), (W * CHUNK, B)], [pltpu.VMEM((ns, P...]
  transfers between devices with their start and end apart: 1 -> 2, of which waited for: 1 -> 1; matrix products, arithmetic and copies ran while one was open for 0% -> 0% of each run, Pallas kernels for 0% -> 1%
where the time goes in v5:
time: 142 us
  blocking collectives  130 us (92%)
  Pallas kernels  4.87 us (3%)
  local copies, waits for them, and re-layouts  2.38 us (2%)
  starting transfers between devices  1.93 us (1%)
  waiting for transfers between devices  1.52 us (1%)
    all_to_all x1, blocking collectives, body(): lax.all_to_all(snapshots, SNAP, split_axis=1, concat_axis=0, tiled=True)  86.2 us
    all_to_all x1, blocking collectives, body(): got = lax.all_to_all(half, PLANE, 0, 0, tiled=True)  24.8 us
    all_to_all x1, blocking collectives, body(): lax.all_to_all(spread.reshape(devices, 1, B), SPREAD, 0, 0, tiled=True)  18.8 us
    pallas_call x1, Pallas kernels, body(): call(gram_kernel, 1, [(W * CHUNK, B), (W * CHUNK, B)], [pltpu.VMEM((ns, P...  2.86 us
  transfers between devices with their start and end apart: 2, of which 1 were waited for; matrix products, arithmetic and copies ran while one was open for 0% of the time, Pallas kernels for 1%

profile of v5, /device:TPU:1, one launch (start us, length us, event | category | flops | bytes accessed | tf_op | source)
XLA Modules:
  0.0 141.5 jit_solution(12533696173883172955)
XLA Ops:
  0.6 2.3 %copy.9 = bf16[4,32,8,1536]{3,2,0,1:T(8,128)(2,1)S(1)} copy(bf16[4,32,8,1536]{3,2,1,0:T(8,128)(2,1)} %bitcast.21) | data formatting | bytes 6291456 | tf_op jit(solution)/shard_map/all_to_all | solution.py:152
  2.9 86.2 %all_to_all.29 = bf16[32,32,1536]{2,0,1:T(8,128)(2,1)S(1)} all-to-all(bf16[32,32,1536]{2,0,1:T(8,128)(2,1)S(1)} %bitcast.19), channel_id=1, replica_groups=mesh['zlo'=2,'y'=4,'x'=4,'zhi'=4,'core'=2] {'x','zhi','core'}, dimensions={1} | all-to-all | bytes 6291456 | tf_op jit(solution)/shard_map/all_to_all | solution.py:152
  89.1 0.0 copy-start
  89.1 2.9 %shard_map.42 = (f32[2304,128]{1,0:T(8,128)S(1)}, f32[2304,128]{1,0:T(8,128)S(1)}) custom-call(bf16[1024,1536]{1,0:T(8,128)(2,1)S(1)} %bitcast.15), custom_call_target="tpu_custom_call" | custom-call | flops 2013265920 | bytes 5505024 | tf_op jit(solution)/shard_map/pallas_call | solution.py:153
  92.0 1.8 %collective-permute-start.1 = (f32[2304,128]{1,0:T(8,128)S(1)}, f32[2304,128]{1,0:T(8,128)S(1)}, u32[]{:S(2)}, u32[]{:S(2)}) collective-permute-start(f32[2304,128]{1,0:T(8,128)S(1)} %get-tuple-element.8), channel_id=1, source_target_pairs={{0,1},{1,0},{2,3},{3,2},{4,5},{5,4},{6,7},{7,6},{8,9},{9,8},{10,11... | collective-permute-start | bytes 3538952 | tf_op jit(solution)/shard_map/ppermute | solution.py:162
  93.8 0.0 copy-done
  93.8 0.7 shard_map.41
  94.5 0.1 collective-permute-start
  94.7 0.1 broadcast_and_fusion.1
  94.7 1.5 %collective-permute-done = f32[1,128]{1,0:T(1,128)S(1)} collective-permute-done((f32[1,128]{1,0:T(1,128)S(1)}, f32[1,128]{1,0:T(1,128)S(1)}, u32[]{:S(2)}, u32[]{:S(2)}) %collective-permute-start) | collective-permute-done | bytes 544 | tf_op jit(solution)/shard_map/ppermute | solution.py:166
  96.3 0.1 fusion.2
  96.3 0.1 maximum_bitcast_fusion
  96.4 0.0 collective-permute-done.1
  96.4 0.1 add.9
  96.5 0.1 select_select_fusion
  96.6 24.8 %all_to_all.30.got_ref = f32[32,72,128]{2,1,0:T(8,128)S(1)} all-to-all(f32[32,72,128]{2,1,0:T(8,128)S(1)} %select_select_fusion), channel_id=1, replica_groups=mesh['zlo'=2,'y'=4,'x'=4,'zhi'=4,'core'=2] {'x','y','zlo'}, dimensions={0} | all-to-all | bytes 2359296 | tf_op jit(solution)/shard_map/all_to_all | solution.py:173
  121.4 0.2 shard_map.43
  121.7 18.8 %all_to_all.31 = f32[256,1,128]{2,1,0:T(1,128)S(1)} all-to-all(f32[256,1,128]{2,1,0:T(1,128)S(1)} %bitcast.18), channel_id=1, replica_groups=mesh['zlo'=2,'y'=4,'x'=4,'zhi'=4,'core'=2] {'x','y','zlo','zhi','core'}, dimensions={0} | all-to-all | bytes 262144 | tf_op jit(solution)/shard_map/all_to_all | solution.py:182
  140.5 1.0 shard_map.44
  (3 shorter events, 0.0 us)
Async XLA Ops:
  89.1 4.7 %copy-start = (bf16[1024,128]{1,0:T(8,128)(2,1)S(1)}, bf16[1024,128]{1,0:T(8,128)(2,1)}, u32[]{:S(2)}) copy-start(bf16[1024,128]{1,0:T(8,128)(2,1)} %coef_ref.1) | copy-start | bytes 786436
  92.0 4.5 %collective-permute-start.1 = (f32[2304,128]{1,0:T(8,128)S(1)}, f32[2304,128]{1,0:T(8,128)S(1)}, u32[]{:S(2)}, u32[]{:S(2)}) collective-permute-start(f32[2304,128]{1,0:T(8,128)S(1)} %get-tuple-element.8), channel_id=1, source_target_pairs={{0,1},{1,0},{2,3},{3,2},{4,5},{5,4},{6,7},{7,6},{8,9},{9,8},{10,11... | collective-permute-start | bytes 3538952 | tf_op jit(solution)/shard_map/ppermute | solution.py:162
  94.5 1.7 %collective-permute-start = (f32[1,128]{1,0:T(1,128)S(1)}, f32[1,128]{1,0:T(1,128)S(1)}, u32[]{:S(2)}, u32[]{:S(2)}) collective-permute-start(f32[1,128]{1,0:T(1,128)S(1)} %get-tuple-element.6), channel_id=1, source_target_pairs={{0,1},{1,0},{2,3},{3,2},{4,5},{5,4},{6,7},{7,6},{8,9},{9,8},{10,11... | collective-permute-start | bytes 1544 | tf_op jit(solution)/shard_map/ppermute | solution.py:166

commit v6 on v5

--- a/solution.py
+++ b/solution.py
@@ -35,12 +35,15 @@
     return lax.broadcasted_iota(jnp.int32, shape, 1) < B // 2
 
 
-def gram_kernel(rows_ref, mine_ref, other_ref, tile_ref):
+def gram_kernel(own, rows_ref, out_ref, tile_ref, left_ref):
     core = lax.axis_index("core")
+    first = (core if own else 1 - core) * W
+    for i in range(NB * 2):
+        left_ref[i * W : (i + 1) * W, :] = rows_ref[pl.ds(pl.multiple_of(2 * i * W + first, W), W), :]
     for sp in range(NB // 2):
-        depth = (sp + 1) * PAIR
+        depth = (sp + 1) * B
         tile_ref[:depth, :] = lax.dot_general(
-            rows_ref[:depth, :],
+            left_ref[:depth, :],
             rows_ref[sp * PAIR : (sp + 1) * PAIR, :],
             (((1,), (1,)), ((), ())),
             preferred_element_type=F32,
@@ -49,13 +52,11 @@
             s = 2 * sp + t
             for a in range(s + 1):
                 for slot in range(2):
-                    top = a * B + slot * 2 * W
                     row = slot * BLOCKS + block(a, s)
-                    for out_ref, c in ((mine_ref, core), (other_ref, 1 - core)):
-                        part = tile_ref[
-                            pl.ds(pl.multiple_of(top + c * W, W), W), t * B : (t + 1) * B
-                        ]
-                        out_ref[pl.ds(row, W, stride=CHUNK), :] = part
+                    top = (2 * a + slot) * W
+                    out_ref[pl.ds(row, W, stride=CHUNK), :] = tile_ref[
+                        top : top + W, t * B : (t + 1) * B
+                    ]
 
 
 def raw_kernel(rows_ref, coef_ref, raw_ref, energy_ref):
@@ -150,19 +151,24 @@
     all_rows = count * lax.axis_size(STATE)
     devices = lax.axis_size(ALL)
     rows = lax.all_to_all(snapshots, SNAP, split_axis=1, concat_axis=0, tiled=True)
-    mine, other = call(
-        gram_kernel,
-        1,
-        [(W * CHUNK, B), (W * CHUNK, B)],
-        [pltpu.VMEM((ns, PAIR), F32)],
-        2 * ns * n * 5 * ns // 8,
-        2 * ns * n + 8 * W * CHUNK * B,
-    )(rows)
+    halves = [
+        call(
+            functools.partial(gram_kernel, own),
+            1,
+            [(W * CHUNK, B)],
+            [pltpu.VMEM((ns // 2, PAIR), F32), pltpu.VMEM((ns // 2, n), rows.dtype)],
+            ns * n * 5 * ns // 8,
+            2 * ns * n + 4 * W * CHUNK * B,
+        )
+        for own in (False, True)
+    ]
     swap = [(i, 1 - i) for i in range(nc)]
+    (other,) = halves[0](rows)
     got = lax.ppermute(other, "core", swap)
     raw, energy = call(
         raw_kernel, 2, [(n, B), (1, B)], [], 2 * ns * n * B, 2 * ns * n + 4 * n * B
     )(rows, coefficients)
+    (mine,) = halves[1](rows)
     energy = energy + lax.ppermute(energy, "core", swap)
     place = lax.broadcasted_iota(jnp.int32, (1, CHUNK, B), 1) - BLOCKS
     left = lax.broadcasted_iota(jnp.int32, (1, CHUNK, B), 2) < B // 2

time: 142 us -> 140 us (0.986)
    pallas_call x1 -> x2, Pallas kernels: 2.86 us -> 2.65 us  [the longest x1 1.33 us: body(): mine, = halves[1](rows)]
where the time goes in v6:
time: 140 us
  blocking collectives  130 us (93%)
  Pallas kernels  4.66 us (3%)
  local copies, waits for them, and re-layouts  2.38 us (2%)
  starting transfers between devices  1.96 us (1%)
    all_to_all x1, blocking collectives, body(): lax.all_to_all(snapshots, SNAP, split_axis=1, concat_axis=0, tiled=True)  86.2 us
    all_to_all x1, blocking collectives, body(): got = lax.all_to_all(half, PLANE, 0, 0, tiled=True)  24.7 us
    all_to_all x1, blocking collectives, body(): lax.all_to_all(spread.reshape(devices, 1, B), SPREAD, 0, 0, tiled=True)  18.8 us
  transfers between devices with their start and end apart: 2, of which 1 were waited for; matrix products, arithmetic and copies ran while one was open for 0% of the time, Pallas kernels for 1%

profile of v6, /device:TPU:1, one launch (start us, length us, event | category | flops | bytes accessed | tf_op | source)
XLA Modules:
  0.0 140.0 jit_solution(3722004504740794671)
XLA Ops:
  0.6 2.3 %copy.9 = bf16[4,32,8,1536]{3,2,0,1:T(8,128)(2,1)S(1)} copy(bf16[4,32,8,1536]{3,2,1,0:T(8,128)(2,1)} %bitcast.22) | data formatting | bytes 6291456 | tf_op jit(solution)/shard_map/all_to_all | solution.py:153
  2.9 86.2 %all_to_all.29 = bf16[32,32,1536]{2,0,1:T(8,128)(2,1)S(1)} all-to-all(bf16[32,32,1536]{2,0,1:T(8,128)(2,1)S(1)} %bitcast.20), channel_id=1, replica_groups=mesh['zlo'=2,'y'=4,'x'=4,'zhi'=4,'core'=2] {'x','zhi','core'}, dimensions={1} | all-to-all | bytes 6291456 | tf_op jit(solution)/shard_map/all_to_all | solution.py:153
  89.1 0.0 copy-start
  89.1 1.3 shard_map.43
  90.4 1.9 %collective-permute-start.1 = (f32[2304,128]{1,0:T(8,128)S(1)}, f32[2304,128]{1,0:T(8,128)S(1)}, u32[]{:S(2)}, u32[]{:S(2)}) collective-permute-start(f32[2304,128]{1,0:T(8,128)S(1)} %shard_map.43), channel_id=1, source_target_pairs={{0,1},{1,0},{2,3},{3,2},{4,5},{5,4},{6,7},{7,6},{8,9},{9,8},{10,11... | collective-permute-start | bytes 3538952 | tf_op jit(solution)/shard_map/ppermute | solution.py:167
  92.3 0.1 broadcast_and_fusion.1
  92.4 0.0 copy-done
  92.4 0.7 shard_map.41
  93.1 0.1 collective-permute-start
  93.2 1.3 shard_map.42
  94.6 0.2 collective-permute-done
  94.8 0.1 fusion.2
  94.8 0.1 maximum_bitcast_fusion
  94.9 0.0 collective-permute-done.1
  94.9 0.1 add.9
  95.0 0.1 select_select_fusion
  95.2 24.7 %all_to_all.30.got_ref = f32[32,72,128]{2,1,0:T(8,128)S(1)} all-to-all(f32[32,72,128]{2,1,0:T(8,128)S(1)} %select_select_fusion), channel_id=1, replica_groups=mesh['zlo'=2,'y'=4,'x'=4,'zhi'=4,'core'=2] {'x','y','zlo'}, dimensions={0} | all-to-all | bytes 2359296 | tf_op jit(solution)/shard_map/all_to_all | solution.py:179
  119.9 0.2 shard_map.44
  120.1 18.8 %all_to_all.31 = f32[256,1,128]{2,1,0:T(1,128)S(1)} all-to-all(f32[256,1,128]{2,1,0:T(1,128)S(1)} %bitcast.19), channel_id=1, replica_groups=mesh['zlo'=2,'y'=4,'x'=4,'zhi'=4,'core'=2] {'x','y','zlo','zhi','core'}, dimensions={0} | all-to-all | bytes 262144 | tf_op jit(solution)/shard_map/all_to_all | solution.py:188
  139.0 1.0 shard_map.45
  (3 shorter events, 0.0 us)
Async XLA Ops:
  89.1 3.3 %copy-start = (bf16[1024,128]{1,0:T(8,128)(2,1)S(1)}, bf16[1024,128]{1,0:T(8,128)(2,1)}, u32[]{:S(2)}) copy-start(bf16[1024,128]{1,0:T(8,128)(2,1)} %coef_ref.1) | copy-start | bytes 786436
  90.4 4.5 %collective-permute-start.1 = (f32[2304,128]{1,0:T(8,128)S(1)}, f32[2304,128]{1,0:T(8,128)S(1)}, u32[]{:S(2)}, u32[]{:S(2)}) collective-permute-start(f32[2304,128]{1,0:T(8,128)S(1)} %shard_map.43), channel_id=1, source_target_pairs={{0,1},{1,0},{2,3},{3,2},{4,5},{5,4},{6,7},{7,6},{8,9},{9,8},{10,11... | collective-permute-start | bytes 3538952 | tf_op jit(solution)/shard_map/ppermute | solution.py:167
  93.1 1.6 %collective-permute-start = (f32[1,128]{1,0:T(1,128)S(1)}, f32[1,128]{1,0:T(1,128)S(1)}, u32[]{:S(2)}, u32[]{:S(2)}) collective-permute-start(f32[1,128]{1,0:T(1,128)S(1)} %get-tuple-element.4), channel_id=1, source_target_pairs={{0,1},{1,0},{2,3},{3,2},{4,5},{5,4},{6,7},{7,6},{8,9},{9,8},{10,11... | collective-permute-start | bytes 1544 | tf_op jit(solution)/shard_map/ppermute | solution.py:172

commit v7 on v6

--- a/solution.py
+++ b/solution.py
@@ -173,7 +173,7 @@
     place = lax.broadcasted_iota(jnp.int32, (1, CHUNK, B), 1) - BLOCKS
     left = lax.broadcasted_iota(jnp.int32, (1, CHUNK, B), 2) < B // 2
     turned = jnp.roll(energy, B // 2, 1)
-    half = (mine + got).reshape(W, CHUNK, B)
+    half = mine.reshape(W, CHUNK, B) + got.reshape(W, CHUNK, B)
     half = jnp.where(left & (place == block(0, 0)), energy[None], half)
     half = jnp.where(left & (place == block(1, 1)), turned[None], half)
     got = lax.all_to_all(half, PLANE, 0, 0, tiled=True)

time: 140 us -> 140 us (level)
  no operation moved by 1% of the time
where the time goes in v7:
time: 140 us
  blocking collectives  130 us (93%)
  Pallas kernels  4.66 us (3%)
  local copies, waits for them, and re-layouts  2.38 us (2%)
  starting transfers between devices  1.96 us (1%)
    all_to_all x1, blocking collectives, body(): lax.all_to_all(snapshots, SNAP, split_axis=1, concat_axis=0, tiled=True)  86.2 us
    all_to_all x1, blocking collectives, body(): got = lax.all_to_all(half, PLANE, 0, 0, tiled=True)  24.7 us
    all_to_all x1, blocking collectives, body(): lax.all_to_all(spread.reshape(devices, 1, B), SPREAD, 0, 0, tiled=True)  18.8 us
  transfers between devices with their start and end apart: 2, of which 1 were waited for; matrix products, arithmetic and copies ran while one was open for 0% of the time, Pallas kernels for 1%

profile of v7, /device:TPU:1, one launch (start us, length us, event | category | flops | bytes accessed | tf_op | source)
XLA Modules:
  0.0 140.0 jit_solution(3722004504740794671)
XLA Ops:
  0.6 2.3 %copy.9 = bf16[4,32,8,1536]{3,2,0,1:T(8,128)(2,1)S(1)} copy(bf16[4,32,8,1536]{3,2,1,0:T(8,128)(2,1)} %bitcast.22) | data formatting | bytes 6291456 | tf_op jit(solution)/shard_map/all_to_all | solution.py:153
  2.9 86.2 %all_to_all.29 = bf16[32,32,1536]{2,0,1:T(8,128)(2,1)S(1)} all-to-all(bf16[32,32,1536]{2,0,1:T(8,128)(2,1)S(1)} %bitcast.20), channel_id=1, replica_groups=mesh['zlo'=2,'y'=4,'x'=4,'zhi'=4,'core'=2] {'x','zhi','core'}, dimensions={1} | all-to-all | bytes 6291456 | tf_op jit(solution)/shard_map/all_to_all | solution.py:153
  89.1 0.0 copy-start
  89.1 1.3 shard_map.43
  90.4 1.9 %collective-permute-start.1 = (f32[2304,128]{1,0:T(8,128)S(1)}, f32[2304,128]{1,0:T(8,128)S(1)}, u32[]{:S(2)}, u32[]{:S(2)}) collective-permute-start(f32[2304,128]{1,0:T(8,128)S(1)} %shard_map.43), channel_id=1, source_target_pairs={{0,1},{1,0},{2,3},{3,2},{4,5},{5,4},{6,7},{7,6},{8,9},{9,8},{10,11... | collective-permute-start | bytes 3538952 | tf_op jit(solution)/shard_map/ppermute | solution.py:167
  92.3 0.1 broadcast_and_fusion.1
  92.4 0.0 copy-done
  92.4 0.7 shard_map.41
  93.1 0.1 collective-permute-start
  93.2 1.3 shard_map.42
  94.6 0.2 collective-permute-done
  94.8 0.1 fusion.2
  94.8 0.1 maximum_bitcast_fusion
  94.9 0.0 collective-permute-done.1
  94.9 0.1 add.12
  95.0 0.1 select_select_fusion
  95.2 24.7 %all_to_all.30.got_ref = f32[32,72,128]{2,1,0:T(8,128)S(1)} all-to-all(f32[32,72,128]{2,1,0:T(8,128)S(1)} %select_select_fusion), channel_id=1, replica_groups=mesh['zlo'=2,'y'=4,'x'=4,'zhi'=4,'core'=2] {'x','y','zlo'}, dimensions={0} | all-to-all | bytes 2359296 | tf_op jit(solution)/shard_map/all_to_all | solution.py:179
  119.9 0.2 shard_map.44
  120.1 18.8 %all_to_all.31 = f32[256,1,128]{2,1,0:T(1,128)S(1)} all-to-all(f32[256,1,128]{2,1,0:T(1,128)S(1)} %bitcast.19), channel_id=1, replica_groups=mesh['zlo'=2,'y'=4,'x'=4,'zhi'=4,'core'=2] {'x','y','zlo','zhi','core'}, dimensions={0} | all-to-all | bytes 262144 | tf_op jit(solution)/shard_map/all_to_all | solution.py:188
  139.0 1.0 shard_map.45
  (3 shorter events, 0.0 us)
Async XLA Ops:
  89.1 3.3 %copy-start = (bf16[1024,128]{1,0:T(8,128)(2,1)S(1)}, bf16[1024,128]{1,0:T(8,128)(2,1)}, u32[]{:S(2)}) copy-start(bf16[1024,128]{1,0:T(8,128)(2,1)} %coef_ref.1) | copy-start | bytes 786436
  90.4 4.5 %collective-permute-start.1 = (f32[2304,128]{1,0:T(8,128)S(1)}, f32[2304,128]{1,0:T(8,128)S(1)}, u32[]{:S(2)}, u32[]{:S(2)}) collective-permute-start(f32[2304,128]{1,0:T(8,128)S(1)} %shard_map.43), channel_id=1, source_target_pairs={{0,1},{1,0},{2,3},{3,2},{4,5},{5,4},{6,7},{7,6},{8,9},{9,8},{10,11... | collective-permute-start | bytes 3538952 | tf_op jit(solution)/shard_map/ppermute | solution.py:167
  93.1 1.6 %collective-permute-start = (f32[1,128]{1,0:T(1,128)S(1)}, f32[1,128]{1,0:T(1,128)S(1)}, u32[]{:S(2)}, u32[]{:S(2)}) collective-permute-start(f32[1,128]{1,0:T(1,128)S(1)} %get-tuple-element.4), channel_id=1, source_target_pairs={{0,1},{1,0},{2,3},{3,2},{4,5},{5,4},{6,7},{7,6},{8,9},{9,8},{10,11... | collective-permute-start | bytes 1544 | tf_op jit(solution)/shard_map/ppermute | solution.py:172
